TPU v7x, 32 devices: a whole 2x2x4 slice. The times are simulated.
32 devices in a mesh: design: 2 (over y), cluster: 4 (over z), blk: 2 (over x), sub: 2 (over core).
Axes of the slice: x: 2, y: 2, z: 4, core: 2. Of those that a mesh axis runs over, the one named last changes fastest.
Arguments:
- density: bfloat16 [16, 256, 256], P(('design', 'cluster')), parts along dimension 0, may hold values from -6 to 6
- far_cols: int32 [256], P(('design', 'cluster', 'blk', 'sub')), parts along dimension 0, may hold values from 0 to 1
- far_bucket: int32 [256], P(('design', 'cluster', 'blk', 'sub')), parts along dimension 0, may hold values from 0 to 4
- far_v: bfloat16 [256, 64, 256], P(('design', 'cluster', 'blk', 'sub')), parts along dimension 0, may hold values from -0.375 to 0.375
- far_u: bfloat16 [256, 64, 256], P(('design', 'cluster', 'blk', 'sub')), parts along dimension 0, may hold values from -0.1875 to 0.1875
- near_rows: int32 [64], P(('design', 'cluster', 'blk', 'sub')), parts along dimension 0, may hold values from 0 to 1
- near_cols: int32 [64], P(('design', 'cluster', 'blk', 'sub')), parts along dimension 0, may hold values from 0 to 5
- near_tiles: bfloat16 [64, 256, 256], P(('design', 'cluster', 'blk', 'sub')), parts along dimension 0, may hold values from -0.125 to 0.125
- ag_leaf: int32 [8192], P(('design', 'cluster', 'blk', 'sub')), parts along dimension 0, may hold values from 0 to 1
- ag_grad: bfloat16 [8192, 3, 256], P(('design', 'cluster', 'blk', 'sub')), parts along dimension 0, may hold values from -0.375 to 0.375
- ag_normal: float32 [6, 4096], P('design', ('cluster', 'blk', 'sub')), parts along dimension 0, may hold values from -5 to 5
- ag_arm: float32 [6, 4096], P('design', ('cluster', 'blk', 'sub')), parts along dimension 0, may hold values from -5 to 5
- ag_area: float32 [8192], P(('design', 'cluster', 'blk', 'sub')), parts along dimension 0, may hold values from 0.002 to 0.02
Outputs:
- potential: bfloat16 [16, 256, 256], P(('design', 'cluster')), parts along dimension 0
- sector_force: float32 [16, 3, 256], P(('design', 'cluster')), parts along dimension 0
- torque: float32 [6, 256], P('design'), parts along dimension 0
There are 2 independent parts, one for each index of `design`. A program takes and returns all parts, laid end to end along the dimension named above; each array names one. Nothing has to cross between parts.
All inputs are finite; a program needn't handle non-finite values.
Results may differ from a plain program's by a relative error of at most 0.0066.
Values may be sent and summed in bfloat16 or wider, within the bound.
A program may use at most 64 MiB of HBM per device.

v0:
```python
import math
import jax
import jax.numpy as jnp
from jax import lax
from jax.sharding import PartitionSpec as P


def padded(block, sides, width):
    for axis, dim in sides:
        count = lax.axis_size(axis)
        forward = [(i, i + 1) for i in range(count - 1)]
        forward.append((count - 1, 0))
        backward = [(target, source) for source, target in forward]
        low = lax.ppermute(
            lax.slice_in_dim(block, block.shape[dim] - width, None, axis=dim), axis, forward
        )
        high = lax.ppermute(lax.slice_in_dim(block, 0, width, axis=dim), axis, backward)
        block = jnp.concatenate([low, block, high], axis=dim)
    return block


def rank_table(bucket, rank_dim):
    widths = rank_dim // jnp.left_shift(jnp.int32(1), 4 - bucket) * (bucket > 0).astype(jnp.int32)
    return jnp.arange(rank_dim, dtype=jnp.int32)[None, :] < widths[:, None]


def surface_stress(phi_local, leaf_ids, grad_rows, normals, arms, areas):
    groups, panels, loads = phi_local.shape
    count = leaf_ids.shape[0]
    field_h = jnp.zeros((count, 3, loads), jnp.float32)
    for leaf_idx in range(groups):
        values = jnp.dot(
            grad_rows.reshape(count * 3, panels),
            phi_local[leaf_idx],
            preferred_element_type=jnp.float32,
        )
        field_h = field_h + jnp.where(
            (leaf_ids == leaf_idx)[:, None, None], values.reshape(count, 3, loads), 0.0
        )
    normal_t = jnp.transpose(normals)[:, :, None]
    along = jnp.sum(field_h * normal_t, axis=1)
    squared = jnp.sum(field_h * field_h, axis=1)
    traction = along[:, None, :] * field_h - 0.5 * squared[:, None, :] * normal_t
    weighted = traction * areas[:, None, None]
    sectors = jnp.stack(
        [
            jnp.sum(jnp.where((leaf_ids == leaf_idx)[:, None, None], weighted, 0.0), axis=0)
            for leaf_idx in range(groups)
        ]
    )
    arm_t = jnp.transpose(arms)[:, :, None]
    moment_x = jnp.sum(arm_t[:, 1] * weighted[:, 2] - arm_t[:, 2] * weighted[:, 1], axis=0)
    moment_y = jnp.sum(arm_t[:, 2] * weighted[:, 0] - arm_t[:, 0] * weighted[:, 2], axis=0)
    moment_z = jnp.sum(arm_t[:, 0] * weighted[:, 1] - arm_t[:, 1] * weighted[:, 0], axis=0)
    return (sectors, jnp.stack([moment_x, moment_y, moment_z]))


def far_field(field, far_cols, far_bucket, far_v, far_u):
    owners = lax.axis_size("cluster")
    groups, panels, loads = field.shape
    rank_dim = far_v.shape[1]
    picked = jnp.take(field, far_cols, axis=0)
    coeffs = jnp.einsum("srl,sln->srn", far_v, picked, preferred_element_type=jnp.float32)
    coeffs = jnp.where(rank_table(far_bucket, rank_dim)[:, :, None], coeffs, 0.0).astype(
        jnp.bfloat16
    )
    coeffs = coeffs.reshape(owners, groups, rank_dim, loads)
    basis = far_u.reshape(owners, groups, rank_dim, panels)
    arrived = lax.all_to_all(coeffs, "cluster", split_axis=0, concat_axis=0, tiled=True)
    return jnp.einsum("bqrl,bqrn->qln", basis, arrived, preferred_element_type=jnp.float32)


def near_field(field, near_rows, near_cols, near_tiles):
    groups = field.shape[0]
    extended = padded(field, (("cluster", 0),), groups)
    picked = jnp.take(extended, near_cols, axis=0)
    values = jnp.einsum("kij,kjn->kin", near_tiles, picked, preferred_element_type=jnp.float32)
    onehot = near_rows[:, None] == jnp.arange(groups, dtype=jnp.int32)[None, :]
    return jnp.sum(jnp.where(onehot[:, :, None, None], values[:, None], 0.0), axis=0)


def apply_operator(field, far_cols, far_bucket, far_v, far_u, near_rows, near_cols, near_tiles):
    partial_sum = far_field(field, far_cols, far_bucket, far_v, far_u) + near_field(
        field, near_rows, near_cols, near_tiles
    )
    summed = lax.psum(partial_sum, ("blk", "sub"))
    return (0.5 * field.astype(jnp.float32) + summed).astype(jnp.bfloat16)


def per_device(
    density,
    far_cols,
    far_bucket,
    far_v,
    far_u,
    near_rows,
    near_cols,
    near_tiles,
    ag_leaf,
    ag_grad,
    ag_normal,
    ag_arm,
    ag_area,
):
    first = apply_operator(
        density, far_cols, far_bucket, far_v, far_u, near_rows, near_cols, near_tiles
    )
    potential = apply_operator(
        first, far_cols, far_bucket, far_v, far_u, near_rows, near_cols, near_tiles
    )
    sector_part, torque_part = surface_stress(
        potential, ag_leaf, ag_grad, ag_normal, ag_arm, ag_area
    )
    scale = 1.0 / math.sqrt(lax.axis_size("cluster") * lax.axis_size("blk") * lax.axis_size("sub"))
    sector_force = lax.psum(sector_part, ("blk", "sub"))
    torque = lax.psum(torque_part, ("cluster", "blk", "sub"))
    return (potential, sector_force, torque * scale)


def solution(mesh):
    placed = (
        P(("design", "cluster"), None, None),
        P(("design", "cluster", "blk", "sub")),
        P(("design", "cluster", "blk", "sub")),
        P(("design", "cluster", "blk", "sub"), None, None),
        P(("design", "cluster", "blk", "sub"), None, None),
        P(("design", "cluster", "blk", "sub")),
        P(("design", "cluster", "blk", "sub")),
        P(("design", "cluster", "blk", "sub"), None, None),
        P(("design", "cluster", "blk", "sub")),
        P(("design", "cluster", "blk", "sub"), None, None),
        P("design", ("cluster", "blk", "sub")),
        P("design", ("cluster", "blk", "sub")),
        P(("design", "cluster", "blk", "sub")),
    )
    return jax.shard_map(
        per_device,
        mesh=mesh,
        in_specs=placed,
        out_specs=(
            P(("design", "cluster"), None, None),
            P(("design", "cluster"), None, None),
            P("design", None),
        ),
        check_vma=False,
    )
```

profile of v0, /device:TPU:0, one launch (start us, length us, event | category | flops | bytes accessed | tf_op | source)
XLA Modules:
  0.0 175.1 jit_solution(4676703497687636807)
XLA Ops:
  7.2 3.1 %collective-permute-start = (bf16[2,256,256]{2,1,0:T(8,128)(2,1)}, bf16[2,256,256]{2,1,0:T(8,128)(2,1)S(1)}, u32[]{:S(2)}, u32[]{:S(2)}) collective-permute-start(bf16[2,256,256]{2,1,0:T(8,128)(2,1)} %param.17), channel_id=1, source_target_pairs={{0,4},{4,8},{8,12},{12,0},{1,5},{5,9},{9,13},{13,1},{2,6},{6,10},{... | collective-permute-start | bytes 786440 | tf_op jit(solution)/shard_map/ppermute | solution.py:14
  10.3 2.1 %collective-permute-start.1 = (bf16[2,256,256]{2,1,0:T(8,128)(2,1)}, bf16[2,256,256]{2,1,0:T(8,128)(2,1)S(1)}, u32[]{:S(2)}, u32[]{:S(2)}) collective-permute-start(bf16[2,256,256]{2,1,0:T(8,128)(2,1)} %param.17), channel_id=1, source_target_pairs={{4,0},{8,4},{12,8},{0,12},{5,1},{9,5},{13,9},{1,13},{6,2},{10,6},{... | collective-permute-start | bytes 786440 | tf_op jit(solution)/shard_map/ppermute | solution.py:17
  12.4 0.7 compare_select_fusion.1
  13.1 1.6 gather_fusion
  14.7 0.1 compare_select_fusion.2
  14.8 0.1 iota_compare_fusion
  14.9 1.1 fusion.12
  16.0 3.5 %all-to-all-start = ((bf16[4,2,64,256]{3,2,1,0:T(8,128)(2,1)}), bf16[4,2,64,256]{3,2,1,0:T(8,128)(2,1)S(1)}, u32[]{:S(2)}, u32[]{:S(2)}) async-start(bf16[4,2,64,256]{3,2,1,0:T(8,128)(2,1)} %bitcast.1), calls=%async_computation | async-start | bytes 524288 | tf_op jit(solution)/shard_map/all_to_all | solution.py:69
  19.7 0.6 copy-done.12
  20.3 0.1 iota_compare_fusion.1
  20.4 4.9 %collective-permute-done.1 = bf16[2,256,256]{2,1,0:T(8,128)(2,1)S(1)} collective-permute-done((bf16[2,256,256]{2,1,0:T(8,128)(2,1)}, bf16[2,256,256]{2,1,0:T(8,128)(2,1)S(1)}, u32[]{:S(2)}, u32[]{:S(2)}) %collective-permute-start.1) | collective-permute-done | bytes 262176 | tf_op jit(solution)/shard_map/ppermute | solution.py:17
  25.3 0.1 pad_maximum_fusion
  25.4 0.6 gather_fusion.1
  26.0 0.4 copy-done.2
  26.4 0.3 convolution_bitcast_fusion.4
  26.7 0.2 copy.67
  26.9 0.1 select_reduce_fusion.3
  27.1 0.2 copy.68
  27.3 2.8 %all-to-all-done = bf16[4,2,64,256]{3,2,1,0:T(8,128)(2,1)S(1)} async-done(((bf16[4,2,64,256]{3,2,1,0:T(8,128)(2,1)}), bf16[4,2,64,256]{3,2,1,0:T(8,128)(2,1)S(1)}, u32[]{:S(2)}, u32[]{:S(2)}) %all-to-all-start) | async-done | bytes 262176 | tf_op jit(solution)/shard_map/all_to_all | solution.py:69
  30.0 1.1 fusion.9
  31.2 0.1 copy.65
  31.3 32.5 %all-reduce.3.cloned.1.call-done = f32[2,256,256]{1,2,0:T(8,128)} async-done(((f32[2,256,256]{1,2,0:T(8,128)}), f32[2,256,256]{1,2,0:T(8,128)}) %all-reduce.3.cloned.1.call-update) | async-done | bytes 524304 | tf_op jit(solution)/shard_map/psum | solution.py:86
  63.8 1.1 add_convert_fusion.1
  64.9 1.5 collective-permute-start.2
  66.4 2.3 %collective-permute-start.3 = (bf16[2,256,256]{1,2,0:T(8,128)(2,1)S(1)}, bf16[2,256,256]{1,2,0:T(8,128)(2,1)S(1)}, u32[]{:S(2)}, u32[]{:S(2)}) collective-permute-start(bf16[2,256,256]{1,2,0:T(8,128)(2,1)S(1)} %add_convert_fusion.1), channel_id=1, source_target_pairs={{4,0},{8,4},{12,8},{0,12},{5,1},{9,5},{13,9},{1,13},{6,2},{10,6},{... | collective-permute-start | bytes 786440 | tf_op jit(solution)/shard_map/ppermute | solution.py:17
  68.7 0.6 gather_fusion.2
  69.4 1.2 fusion.11
  70.6 3.4 %all-to-all-start.1 = ((bf16[4,2,64,256]{3,2,1,0:T(8,128)(2,1)}), bf16[4,2,64,256]{3,2,1,0:T(8,128)(2,1)S(1)}, u32[]{:S(2)}, u32[]{:S(2)}) async-start(bf16[4,2,64,256]{3,2,1,0:T(8,128)(2,1)} %bitcast.7), calls=%async_computation.1 | async-start | bytes 524288 | tf_op jit(solution)/shard_map/all_to_all | solution.py:69
  74.0 0.0 all-reduce.5.cloned.1.call-start
  74.0 1.9 %collective-permute-done.2 = bf16[2,256,256]{1,2,0:T(8,128)(2,1)S(1)} collective-permute-done((bf16[2,256,256]{1,2,0:T(8,128)(2,1)S(1)}, bf16[2,256,256]{1,2,0:T(8,128)(2,1)S(1)}, u32[]{:S(2)}, u32[]{:S(2)}) %collective-permute-start.2) | collective-permute-done | bytes 262176 | tf_op jit(solution)/shard_map/ppermute | solution.py:14
  76.0 4.2 %collective-permute-done.3 = bf16[2,256,256]{1,2,0:T(8,128)(2,1)S(1)} collective-permute-done((bf16[2,256,256]{1,2,0:T(8,128)(2,1)S(1)}, bf16[2,256,256]{1,2,0:T(8,128)(2,1)S(1)}, u32[]{:S(2)}, u32[]{:S(2)}) %collective-permute-start.3) | collective-permute-done | bytes 262176 | tf_op jit(solution)/shard_map/ppermute | solution.py:17
  80.2 0.1 pad_maximum_fusion.1
  80.3 0.6 gather_fusion.3
  80.8 0.3 convolution_bitcast_fusion.2
  81.1 0.2 copy.70
  81.3 0.1 select_reduce_fusion.2
  81.4 0.2 copy.71
  81.7 3.2 %all-to-all-done.1 = bf16[4,2,64,256]{3,2,1,0:T(8,128)(2,1)S(1)} async-done(((bf16[4,2,64,256]{3,2,1,0:T(8,128)(2,1)}), bf16[4,2,64,256]{3,2,1,0:T(8,128)(2,1)S(1)}, u32[]{:S(2)}, u32[]{:S(2)}) %all-to-all-start.1) | async-done | bytes 262176 | tf_op jit(solution)/shard_map/all_to_all | solution.py:69
  84.9 1.1 fusion.10
  86.0 0.7 copy-done.6
  86.7 0.3 copy-done.3
  87.0 0.3 copy.72
  87.3 0.3 reshape.95
  87.7 0.3 copy-done.4
  88.0 0.1 copy.75
  88.1 0.5 copy-done.5
  88.7 29.0 %all-reduce.5.cloned.1.call-done = f32[2,256,256]{1,2,0:T(8,128)} async-done(((f32[2,256,256]{1,2,0:T(8,128)}), f32[2,256,256]{1,2,0:T(8,128)}) %all-reduce.5.cloned.1.call-update) | async-done | bytes 524304 | tf_op jit(solution)/shard_map/psum | solution.py:86
  117.7 1.1 add_convert_fusion
  118.8 0.3 convolution_bitcast_fusion.1
  119.1 1.2 convolution_bitcast_fusion
  120.3 0.8 copy.77
  121.1 0.3 copy.73
  121.4 0.3 reshape.96
  121.7 1.4 copy.74
  123.1 0.3 reshape.97
  123.5 2.9 %multiply_reduce_fusion.1 = (f32[256,256]{1,0:T(8,128)S(1)}, f32[256,3,256]{2,1,0:T(4,128)S(1)}) fusion(f32[256,3,256]{2,1,0:T(4,128)S(1)} %reshape.97, pred[256]{0:T(512)(128)(4,1)S(1)} %get-tuple-element.31, f32[256,3,256]{2,1,0:T(4,128)S(1)} %reshape.96, pred[256]{0:T(512)(128)(4,1)S(1)} %get-tuple-element.30), kind=kLoop, calls=%fused_computation.26 | loop fusion | flops 917504 | bytes 2621952 | tf_op jit(solution)/shard_map/reduce_sum | solution.py:42
  126.5 0.7 copy-done.8
  127.1 1.9 %select_reduce_fusion.1 = (f32[3,256]{1,0:T(4,128)S(1)}, f32[3,256]{1,0:T(4,128)S(1)}, f32[256,3,256]{2,1,0:T(4,128)S(1)}) fusion(pred[256]{0:T(512)(128)(4,1)S(1)} %get-tuple-element.30, pred[256]{0:T(512)(128)(4,1)S(1)} %get-tuple-element.31, f32[256]{0:T(256)S(1)} %copy-done.8, f32[256,3]{1,0:T(8,128)S(1)} %copy.75, ...), kind=kOutput, calls=%fused_computation.25 | output fusion | flops 1833474 | bytes 1845760 | tf_op jit(solution)/shard_map/mul | solution.py:43
  129.1 0.5 fusion.36
  129.6 0.2 fusion.25
  129.8 31.3 %psum.31 = f32[3,256]{1,0:T(4,128)S(1)} all-reduce(f32[3,256]{1,0:T(4,128)S(1)} %pad_maximum_fusion.3), channel_id=1, replica_groups=mesh['design'=2,'cluster'=4,'blk'=2,'sub'=2] {'cluster','blk','sub'}, use_global_device_ids=true, to_apply=%region_12.15 | all-reduce | flops 768 | bytes 6144 | tf_op jit(solution)/shard_map/psum | solution.py:116
  161.2 0.6 broadcast_multiply_fusion.1
  161.8 5.8 %psum.30 = f32[2,3,256]{2,1,0:T(4,128)S(1)} all-reduce(f32[2,3,256]{2,1,0:T(4,128)S(1)} %pad_maximum_fusion.2), channel_id=1, replica_groups=mesh['design'=2,'cluster'=4,'blk'=2,'sub'=2] {'blk','sub'}, use_global_device_ids=true, to_apply=%region_8.11 | all-reduce | flops 1536 | bytes 12288 | tf_op jit(solution)/shard_map/psum | solution.py:115
  167.6 0.6 copy.78
  (33 shorter events, 0.2 us)
Async XLA Ops:
  7.2 22.9 %copy-start = (bf16[8,64,256]{2,1,0:T(8,128)(2,1)S(1)}, bf16[8,64,256]{2,1,0:T(8,128)(2,1)}, u32[]{:S(2)}) copy-start(bf16[8,64,256]{2,1,0:T(8,128)(2,1)} %param.21) | copy-start | bytes 786436
  7.2 5.8 %copy-start.9 = (s32[8]{0:T(128)S(1)}, s32[8]{0:T(128)}, u32[]{:S(2)}) copy-start(s32[8]{0:T(128)} %param.18) | copy-start | bytes 100
  7.2 13.2 %collective-permute-start = (bf16[2,256,256]{2,1,0:T(8,128)(2,1)}, bf16[2,256,256]{2,1,0:T(8,128)(2,1)S(1)}, u32[]{:S(2)}, u32[]{:S(2)}) collective-permute-start(bf16[2,256,256]{2,1,0:T(8,128)(2,1)} %param.17), channel_id=1, source_target_pairs={{0,4},{4,8},{8,12},{12,0},{1,5},{5,9},{9,13},{13,1},{2,6},{6,10},{... | collective-permute-start | bytes 786440 | tf_op jit(solution)/shard_map/ppermute | solution.py:14
  10.3 15.1 %collective-permute-start.1 = (bf16[2,256,256]{2,1,0:T(8,128)(2,1)}, bf16[2,256,256]{2,1,0:T(8,128)(2,1)S(1)}, u32[]{:S(2)}, u32[]{:S(2)}) collective-permute-start(bf16[2,256,256]{2,1,0:T(8,128)(2,1)} %param.17), channel_id=1, source_target_pairs={{4,0},{8,4},{12,8},{0,12},{5,1},{9,5},{13,9},{1,13},{6,2},{10,6},{... | collective-permute-start | bytes 786440 | tf_op jit(solution)/shard_map/ppermute | solution.py:17
  13.0 1.6 copy-start.10
  13.1 1.8 %copy-start.7 = (bf16[8,64,256]{2,1,0:T(8,128)(2,1)S(1)}, bf16[8,64,256]{2,1,0:T(8,128)(2,1)}, u32[]{:S(2)}) copy-start(bf16[8,64,256]{2,1,0:T(8,128)(2,1)} %param.20) | copy-start | bytes 786436
  16.0 3.6 %copy-start.11 = (s32[2]{0:T(128)S(1)}, s32[2]{0:T(128)}, u32[]{:S(2)}) copy-start(s32[2]{0:T(128)} %param.23) | copy-start | bytes 28
  16.0 9.3 %copy-start.1 = (bf16[2,256,256]{2,1,0:T(8,128)(2,1)S(1)}, bf16[2,256,256]{2,1,0:T(8,128)(2,1)}, u32[]{:S(2)}) copy-start(bf16[2,256,256]{2,1,0:T(8,128)(2,1)} %param.17) | copy-start | bytes 786436
  16.0 14.0 %all-to-all-start = ((bf16[4,2,64,256]{3,2,1,0:T(8,128)(2,1)}), bf16[4,2,64,256]{3,2,1,0:T(8,128)(2,1)S(1)}, u32[]{:S(2)}, u32[]{:S(2)}) async-start(bf16[4,2,64,256]{3,2,1,0:T(8,128)(2,1)} %bitcast.1), calls=%async_computation | async-start | bytes 524288 | tf_op jit(solution)/shard_map/all_to_all | solution.py:69
  19.6 44.2 %all-reduce.3.cloned.1.call-start = ((), (), s32[]{:S(2)}) async-start(), calls=%async_computation.2 | async-start | bytes 1048576 | tf_op jit(solution)/shard_map/psum | solution.py:86
  19.7 0.7 copy-start.12
  25.4 1.0 copy-start.2
  64.9 11.1 %collective-permute-start.2 = (bf16[2,256,256]{1,2,0:T(8,128)(2,1)S(1)}, bf16[2,256,256]{1,2,0:T(8,128)(2,1)S(1)}, u32[]{:S(2)}, u32[]{:S(2)}) collective-permute-start(bf16[2,256,256]{1,2,0:T(8,128)(2,1)S(1)} %add_convert_fusion.1), channel_id=1, source_target_pairs={{0,4},{4,8},{8,12},{12,0},{1,5},{5,9},{9,13},{13,1},{2,6},{6,10},{... | collective-permute-start | bytes 786440 | tf_op jit(solution)/shard_map/ppermute | solution.py:14
  66.4 13.8 %collective-permute-start.3 = (bf16[2,256,256]{1,2,0:T(8,128)(2,1)S(1)}, bf16[2,256,256]{1,2,0:T(8,128)(2,1)S(1)}, u32[]{:S(2)}, u32[]{:S(2)}) collective-permute-start(bf16[2,256,256]{1,2,0:T(8,128)(2,1)S(1)} %add_convert_fusion.1), channel_id=1, source_target_pairs={{4,0},{8,4},{12,8},{0,12},{5,1},{9,5},{13,9},{1,13},{6,2},{10,6},{... | collective-permute-start | bytes 786440 | tf_op jit(solution)/shard_map/ppermute | solution.py:17
  70.6 14.3 %all-to-all-start.1 = ((bf16[4,2,64,256]{3,2,1,0:T(8,128)(2,1)}), bf16[4,2,64,256]{3,2,1,0:T(8,128)(2,1)S(1)}, u32[]{:S(2)}, u32[]{:S(2)}) async-start(bf16[4,2,64,256]{3,2,1,0:T(8,128)(2,1)} %bitcast.7), calls=%async_computation.1 | async-start | bytes 524288 | tf_op jit(solution)/shard_map/all_to_all | solution.py:69
  74.0 43.7 %all-reduce.5.cloned.1.call-start = ((), (), s32[]{:S(2)}) async-start(), calls=%async_computation.3 | async-start | bytes 1048576 | tf_op jit(solution)/shard_map/psum | solution.py:86
  86.0 1.0 copy-start.3
  86.0 0.7 copy-start.6
  87.3 0.7 copy-start.4
  88.0 0.7 copy-start.5
  126.4 0.7 copy-start.8
Sparse Core Ops, SparseCore 0:
  31.3 32.4 all-reduce.2
  86.1 31.5 all-reduce.4
where the time goes:
time: 176 us; the launch traced here: 175 us
  waiting for transfers between devices  78.5 us (45%)
  blocking collectives  37.2 us (21%)
  starting transfers between devices  16.1 us (9%)
  between operations  14.4 us (8%)
  local copies, waits for them, and re-layouts  13 us (7%)
  other arithmetic  9.29 us (5%)
  matrix products  6.61 us (4%)
    psum x2, waiting for transfers between devices, apply_operator(): summed = lax.psum(partial_sum, ('blk', 'sub'))  61.5 us
    psum x1, blocking collectives, per_device(): torque = lax.psum(torque_part, ('cluster', 'blk', 'sub'))  31.3 us
    ppermute x2, waiting for transfers between devices, padded(): lax.ppermute(lax.slice_in_dim(block, 0, width, axis=dim), axis, backward)  9.12 us
    all_to_all x2, starting transfers between devices, far_field(): lax.all_to_all(coeffs, 'cluster', split_axis=0, concat_axis=0, tiled=True)  6.95 us
    all_to_all x2, waiting for transfers between devices, far_field(): lax.all_to_all(coeffs, 'cluster', split_axis=0, concat_axis=0, tiled=True)  5.97 us
    psum x1, blocking collectives, per_device(): sector_force = lax.psum(sector_part, ('blk', 'sub'))  5.84 us
    unnamed x30, local copies, waits for them, and re-layouts  5.5 us
    ppermute x2, starting transfers between devices, padded(): lax.ppermute(lax.slice_in_dim(block, block.shape[dim] - width, None, axis...  4.62 us
  transfers between devices with their start and end apart: 8, of which 7 were waited for; matrix products, arithmetic and copies ran while one was open for 5% of the time, Pallas kernels for 0%

commit v1 on v0

--- a/solution.py
+++ b/solution.py
@@ -112,7 +112,8 @@
         potential, ag_leaf, ag_grad, ag_normal, ag_arm, ag_area
     )
     scale = 1.0 / math.sqrt(lax.axis_size("cluster") * lax.axis_size("blk") * lax.axis_size("sub"))
-    sector_force = lax.psum(sector_part, ("blk", "sub"))
+    parts = lax.all_gather(sector_part, ("blk", "sub"), axis=0, tiled=False)
+    sector_force = parts.sum(axis=0)
     torque = lax.psum(torque_part, ("cluster", "blk", "sub"))
     return (potential, sector_force, torque * scale)
 

time: 176 us -> 175 us (level)
    psum x1 -> x0, blocking collectives: 5.84 us -> none  [per_device(): sector_force = lax.psum(sector_part, ('blk', 'sub'))]
    all_gather x0 -> x1, blocking collectives: none -> 5.18 us  [per_device(): parts = lax.all_gather(sector_part, ('blk', 'sub'), axis=0, tiled=False)]
where the time goes in v1:
time: 175 us; the launch traced here: 174 us
  waiting for transfers between devices  78.5 us (45%)
  blocking collectives  36.5 us (21%)
  starting transfers between devices  16.1 us (9%)
  between operations  14.4 us (8%)
  local copies, waits for them, and re-layouts  13 us (7%)
  other arithmetic  9.31 us (5%)
  matrix products  6.61 us (4%)
    psum x2, waiting for transfers between devices, apply_operator(): summed = lax.psum(partial_sum, ('blk', 'sub'))  61.5 us
    psum x1, blocking collectives, per_device(): torque = lax.psum(torque_part, ('cluster', 'blk', 'sub'))  31.3 us
    ppermute x2, waiting for transfers between devices, padded(): lax.ppermute(lax.slice_in_dim(block, 0, width, axis=dim), axis, backward)  9.12 us
    all_to_all x2, starting transfers between devices, far_field(): lax.all_to_all(coeffs, 'cluster', split_axis=0, concat_axis=0, tiled=True)  6.95 us
    all_to_all x2, waiting for transfers between devices, far_field(): lax.all_to_all(coeffs, 'cluster', split_axis=0, concat_axis=0, tiled=True)  5.97 us
    unnamed x30, local copies, waits for them, and re-layouts  5.5 us
    all_gather x1, blocking collectives, per_device(): parts = lax.all_gather(sector_part, ('blk', 'sub'), axis=0, tiled=False)  5.18 us
    ppermute x2, starting transfers between devices, padded(): lax.ppermute(lax.slice_in_dim(block, block.shape[dim] - width, None, axis...  4.62 us
  transfers between devices with their start and end apart: 8, of which 7 were waited for; matrix products, arithmetic and copies ran while one was open for 5% of the time, Pallas kernels for 0%

profile of v1, /device:TPU:0, one launch (start us, length us, event | category | flops | bytes accessed | tf_op | source)
XLA Modules:
  0.0 174.4 jit_solution(17010260839504503311)
XLA Ops:
  7.2 3.1 %collective-permute-start = (bf16[2,256,256]{2,1,0:T(8,128)(2,1)}, bf16[2,256,256]{2,1,0:T(8,128)(2,1)S(1)}, u32[]{:S(2)}, u32[]{:S(2)}) collective-permute-start(bf16[2,256,256]{2,1,0:T(8,128)(2,1)} %param.17), channel_id=1, source_target_pairs={{0,4},{4,8},{8,12},{12,0},{1,5},{5,9},{9,13},{13,1},{2,6},{6,10},{... | collective-permute-start | bytes 786440 | tf_op jit(solution)/shard_map/ppermute | solution.py:14
  10.3 2.1 %collective-permute-start.1 = (bf16[2,256,256]{2,1,0:T(8,128)(2,1)}, bf16[2,256,256]{2,1,0:T(8,128)(2,1)S(1)}, u32[]{:S(2)}, u32[]{:S(2)}) collective-permute-start(bf16[2,256,256]{2,1,0:T(8,128)(2,1)} %param.17), channel_id=1, source_target_pairs={{4,0},{8,4},{12,8},{0,12},{5,1},{9,5},{13,9},{1,13},{6,2},{10,6},{... | collective-permute-start | bytes 786440 | tf_op jit(solution)/shard_map/ppermute | solution.py:17
  12.4 0.7 compare_select_fusion.1
  13.1 1.6 gather_fusion
  14.7 0.1 compare_select_fusion.2
  14.8 0.1 iota_compare_fusion
  14.9 1.1 fusion.12
  16.0 3.5 %all-to-all-start = ((bf16[4,2,64,256]{3,2,1,0:T(8,128)(2,1)}), bf16[4,2,64,256]{3,2,1,0:T(8,128)(2,1)S(1)}, u32[]{:S(2)}, u32[]{:S(2)}) async-start(bf16[4,2,64,256]{3,2,1,0:T(8,128)(2,1)} %bitcast.1), calls=%async_computation | async-start | bytes 524288 | tf_op jit(solution)/shard_map/all_to_all | solution.py:69
  19.7 0.6 copy-done.12
  20.3 0.1 iota_compare_fusion.1
  20.4 4.9 %collective-permute-done.1 = bf16[2,256,256]{2,1,0:T(8,128)(2,1)S(1)} collective-permute-done((bf16[2,256,256]{2,1,0:T(8,128)(2,1)}, bf16[2,256,256]{2,1,0:T(8,128)(2,1)S(1)}, u32[]{:S(2)}, u32[]{:S(2)}) %collective-permute-start.1) | collective-permute-done | bytes 262176 | tf_op jit(solution)/shard_map/ppermute | solution.py:17
  25.3 0.1 pad_maximum_fusion
  25.4 0.6 gather_fusion.1
  26.0 0.4 copy-done.2
  26.4 0.3 convolution_bitcast_fusion.4
  26.7 0.2 copy.77
  26.9 0.1 select_reduce_fusion.3
  27.1 0.2 copy.78
  27.3 2.8 %all-to-all-done = bf16[4,2,64,256]{3,2,1,0:T(8,128)(2,1)S(1)} async-done(((bf16[4,2,64,256]{3,2,1,0:T(8,128)(2,1)}), bf16[4,2,64,256]{3,2,1,0:T(8,128)(2,1)S(1)}, u32[]{:S(2)}, u32[]{:S(2)}) %all-to-all-start) | async-done | bytes 262176 | tf_op jit(solution)/shard_map/all_to_all | solution.py:69
  30.0 1.1 fusion.9
  31.2 0.1 copy.75
  31.3 32.5 %all-reduce.3.cloned.1.call-done = f32[2,256,256]{1,2,0:T(8,128)} async-done(((f32[2,256,256]{1,2,0:T(8,128)}), f32[2,256,256]{1,2,0:T(8,128)}) %all-reduce.3.cloned.1.call-update) | async-done | bytes 524304 | tf_op jit(solution)/shard_map/psum | solution.py:86
  63.8 1.1 add_convert_fusion.1
  64.9 1.5 collective-permute-start.2
  66.4 2.3 %collective-permute-start.3 = (bf16[2,256,256]{1,2,0:T(8,128)(2,1)S(1)}, bf16[2,256,256]{1,2,0:T(8,128)(2,1)S(1)}, u32[]{:S(2)}, u32[]{:S(2)}) collective-permute-start(bf16[2,256,256]{1,2,0:T(8,128)(2,1)S(1)} %add_convert_fusion.1), channel_id=1, source_target_pairs={{4,0},{8,4},{12,8},{0,12},{5,1},{9,5},{13,9},{1,13},{6,2},{10,6},{... | collective-permute-start | bytes 786440 | tf_op jit(solution)/shard_map/ppermute | solution.py:17
  68.7 0.6 gather_fusion.2
  69.4 1.2 fusion.11
  70.6 3.4 %all-to-all-start.1 = ((bf16[4,2,64,256]{3,2,1,0:T(8,128)(2,1)}), bf16[4,2,64,256]{3,2,1,0:T(8,128)(2,1)S(1)}, u32[]{:S(2)}, u32[]{:S(2)}) async-start(bf16[4,2,64,256]{3,2,1,0:T(8,128)(2,1)} %bitcast.7), calls=%async_computation.1 | async-start | bytes 524288 | tf_op jit(solution)/shard_map/all_to_all | solution.py:69
  74.0 0.0 all-reduce.5.cloned.1.call-start
  74.0 1.9 %collective-permute-done.2 = bf16[2,256,256]{1,2,0:T(8,128)(2,1)S(1)} collective-permute-done((bf16[2,256,256]{1,2,0:T(8,128)(2,1)S(1)}, bf16[2,256,256]{1,2,0:T(8,128)(2,1)S(1)}, u32[]{:S(2)}, u32[]{:S(2)}) %collective-permute-start.2) | collective-permute-done | bytes 262176 | tf_op jit(solution)/shard_map/ppermute | solution.py:14
  76.0 4.2 %collective-permute-done.3 = bf16[2,256,256]{1,2,0:T(8,128)(2,1)S(1)} collective-permute-done((bf16[2,256,256]{1,2,0:T(8,128)(2,1)S(1)}, bf16[2,256,256]{1,2,0:T(8,128)(2,1)S(1)}, u32[]{:S(2)}, u32[]{:S(2)}) %collective-permute-start.3) | collective-permute-done | bytes 262176 | tf_op jit(solution)/shard_map/ppermute | solution.py:17
  80.2 0.1 pad_maximum_fusion.1
  80.3 0.6 gather_fusion.3
  80.8 0.3 convolution_bitcast_fusion.2
  81.1 0.2 copy.80
  81.3 0.1 select_reduce_fusion.2
  81.4 0.2 copy.81
  81.7 3.2 %all-to-all-done.1 = bf16[4,2,64,256]{3,2,1,0:T(8,128)(2,1)S(1)} async-done(((bf16[4,2,64,256]{3,2,1,0:T(8,128)(2,1)}), bf16[4,2,64,256]{3,2,1,0:T(8,128)(2,1)S(1)}, u32[]{:S(2)}, u32[]{:S(2)}) %all-to-all-start.1) | async-done | bytes 262176 | tf_op jit(solution)/shard_map/all_to_all | solution.py:69
  84.9 1.1 fusion.10
  86.0 0.7 copy-done.6
  86.7 0.3 copy-done.3
  87.0 0.3 copy.82
  87.3 0.3 reshape.95
  87.7 0.3 copy-done.4
  88.0 0.1 copy.85
  88.1 0.5 copy-done.5
  88.7 29.0 %all-reduce.5.cloned.1.call-done = f32[2,256,256]{1,2,0:T(8,128)} async-done(((f32[2,256,256]{1,2,0:T(8,128)}), f32[2,256,256]{1,2,0:T(8,128)}) %all-reduce.5.cloned.1.call-update) | async-done | bytes 524304 | tf_op jit(solution)/shard_map/psum | solution.py:86
  117.7 1.1 add_convert_fusion
  118.8 0.3 convolution_bitcast_fusion.1
  119.1 1.2 convolution_bitcast_fusion
  120.3 0.8 copy.87
  121.1 0.3 copy.83
  121.4 0.3 reshape.96
  121.7 1.4 copy.84
  123.1 0.3 reshape.97
  123.5 2.9 %multiply_reduce_fusion.1 = (f32[256,256]{1,0:T(8,128)S(1)}, f32[256,3,256]{2,1,0:T(4,128)S(1)}) fusion(f32[256,3,256]{2,1,0:T(4,128)S(1)} %reshape.97, pred[256]{0:T(512)(128)(4,1)S(1)} %get-tuple-element.34, f32[256,3,256]{2,1,0:T(4,128)S(1)} %reshape.96, pred[256]{0:T(512)(128)(4,1)S(1)} %get-tuple-element.33), kind=kLoop, calls=%fused_computation.26 | loop fusion | flops 917504 | bytes 2621952 | tf_op jit(solution)/shard_map/reduce_sum | solution.py:42
  126.5 0.7 copy-done.8
  127.1 1.9 %select_reduce_fusion.1 = (f32[3,256]{1,0:T(4,128)S(1)}, f32[3,256]{1,0:T(4,128)S(1)}, f32[256,3,256]{2,1,0:T(4,128)S(1)}) fusion(pred[256]{0:T(512)(128)(4,1)S(1)} %get-tuple-element.33, pred[256]{0:T(512)(128)(4,1)S(1)} %get-tuple-element.34, f32[256]{0:T(256)S(1)} %copy-done.8, f32[256,3]{1,0:T(8,128)S(1)} %copy.85, ...), kind=kOutput, calls=%fused_computation.25 | output fusion | flops 1833474 | bytes 1845760 | tf_op jit(solution)/shard_map/mul | solution.py:43
  129.1 0.5 fusion.36
  129.6 0.2 fusion.25
  129.8 31.3 %psum.23 = f32[3,256]{1,0:T(4,128)S(1)} all-reduce(f32[3,256]{1,0:T(4,128)S(1)} %pad_maximum_fusion.3), channel_id=1, replica_groups=mesh['design'=2,'cluster'=4,'blk'=2,'sub'=2] {'cluster','blk','sub'}, use_global_device_ids=true, to_apply=%region_12.15 | all-reduce | flops 768 | bytes 6144 | tf_op jit(solution)/shard_map/psum | solution.py:117
  161.2 0.6 broadcast_multiply_fusion.1
  161.8 5.2 %all-gather = f32[8,3,256]{2,1,0:T(4,128)S(1)} all-gather(f32[2,3,256]{2,1,0:T(4,128)S(1)} %pad_maximum_fusion.2), channel_id=2, replica_groups=mesh['design'=2,'cluster'=4,'blk'=2,'sub'=2] {'blk','sub'}, dimensions={0}, use_global_device_ids=true | all-gather | bytes 30720 | tf_op jit(solution)/shard_map/all_gather | solution.py:115
  167.0 0.6 copy.88
  (34 shorter events, 0.2 us)
Async XLA Ops:
  7.2 22.9 %copy-start = (bf16[8,64,256]{2,1,0:T(8,128)(2,1)S(1)}, bf16[8,64,256]{2,1,0:T(8,128)(2,1)}, u32[]{:S(2)}) copy-start(bf16[8,64,256]{2,1,0:T(8,128)(2,1)} %param.21) | copy-start | bytes 786436
  7.2 5.8 %copy-start.9 = (s32[8]{0:T(128)S(1)}, s32[8]{0:T(128)}, u32[]{:S(2)}) copy-start(s32[8]{0:T(128)} %param.18) | copy-start | bytes 100
  7.2 13.2 %collective-permute-start = (bf16[2,256,256]{2,1,0:T(8,128)(2,1)}, bf16[2,256,256]{2,1,0:T(8,128)(2,1)S(1)}, u32[]{:S(2)}, u32[]{:S(2)}) collective-permute-start(bf16[2,256,256]{2,1,0:T(8,128)(2,1)} %param.17), channel_id=1, source_target_pairs={{0,4},{4,8},{8,12},{12,0},{1,5},{5,9},{9,13},{13,1},{2,6},{6,10},{... | collective-permute-start | bytes 786440 | tf_op jit(solution)/shard_map/ppermute | solution.py:14
  10.3 15.1 %collective-permute-start.1 = (bf16[2,256,256]{2,1,0:T(8,128)(2,1)}, bf16[2,256,256]{2,1,0:T(8,128)(2,1)S(1)}, u32[]{:S(2)}, u32[]{:S(2)}) collective-permute-start(bf16[2,256,256]{2,1,0:T(8,128)(2,1)} %param.17), channel_id=1, source_target_pairs={{4,0},{8,4},{12,8},{0,12},{5,1},{9,5},{13,9},{1,13},{6,2},{10,6},{... | collective-permute-start | bytes 786440 | tf_op jit(solution)/shard_map/ppermute | solution.py:17
  13.0 1.6 copy-start.10
  13.1 1.8 %copy-start.7 = (bf16[8,64,256]{2,1,0:T(8,128)(2,1)S(1)}, bf16[8,64,256]{2,1,0:T(8,128)(2,1)}, u32[]{:S(2)}) copy-start(bf16[8,64,256]{2,1,0:T(8,128)(2,1)} %param.20) | copy-start | bytes 786436
  16.0 3.6 %copy-start.11 = (s32[2]{0:T(128)S(1)}, s32[2]{0:T(128)}, u32[]{:S(2)}) copy-start(s32[2]{0:T(128)} %param.23) | copy-start | bytes 28
  16.0 9.3 %copy-start.1 = (bf16[2,256,256]{2,1,0:T(8,128)(2,1)S(1)}, bf16[2,256,256]{2,1,0:T(8,128)(2,1)}, u32[]{:S(2)}) copy-start(bf16[2,256,256]{2,1,0:T(8,128)(2,1)} %param.17) | copy-start | bytes 786436
  16.0 14.0 %all-to-all-start = ((bf16[4,2,64,256]{3,2,1,0:T(8,128)(2,1)}), bf16[4,2,64,256]{3,2,1,0:T(8,128)(2,1)S(1)}, u32[]{:S(2)}, u32[]{:S(2)}) async-start(bf16[4,2,64,256]{3,2,1,0:T(8,128)(2,1)} %bitcast.1), calls=%async_computation | async-start | bytes 524288 | tf_op jit(solution)/shard_map/all_to_all | solution.py:69
  19.6 44.2 %all-reduce.3.cloned.1.call-start = ((), (), s32[]{:S(2)}) async-start(), calls=%async_computation.2 | async-start | bytes 1048576 | tf_op jit(solution)/shard_map/psum | solution.py:86
  19.7 0.7 copy-start.12
  25.4 1.0 copy-start.2
  64.9 11.1 %collective-permute-start.2 = (bf16[2,256,256]{1,2,0:T(8,128)(2,1)S(1)}, bf16[2,256,256]{1,2,0:T(8,128)(2,1)S(1)}, u32[]{:S(2)}, u32[]{:S(2)}) collective-permute-start(bf16[2,256,256]{1,2,0:T(8,128)(2,1)S(1)} %add_convert_fusion.1), channel_id=1, source_target_pairs={{0,4},{4,8},{8,12},{12,0},{1,5},{5,9},{9,13},{13,1},{2,6},{6,10},{... | collective-permute-start | bytes 786440 | tf_op jit(solution)/shard_map/ppermute | solution.py:14
  66.4 13.8 %collective-permute-start.3 = (bf16[2,256,256]{1,2,0:T(8,128)(2,1)S(1)}, bf16[2,256,256]{1,2,0:T(8,128)(2,1)S(1)}, u32[]{:S(2)}, u32[]{:S(2)}) collective-permute-start(bf16[2,256,256]{1,2,0:T(8,128)(2,1)S(1)} %add_convert_fusion.1), channel_id=1, source_target_pairs={{4,0},{8,4},{12,8},{0,12},{5,1},{9,5},{13,9},{1,13},{6,2},{10,6},{... | collective-permute-start | bytes 786440 | tf_op jit(solution)/shard_map/ppermute | solution.py:17
  70.6 14.3 %all-to-all-start.1 = ((bf16[4,2,64,256]{3,2,1,0:T(8,128)(2,1)}), bf16[4,2,64,256]{3,2,1,0:T(8,128)(2,1)S(1)}, u32[]{:S(2)}, u32[]{:S(2)}) async-start(bf16[4,2,64,256]{3,2,1,0:T(8,128)(2,1)} %bitcast.7), calls=%async_computation.1 | async-start | bytes 524288 | tf_op jit(solution)/shard_map/all_to_all | solution.py:69
  74.0 43.7 %all-reduce.5.cloned.1.call-start = ((), (), s32[]{:S(2)}) async-start(), calls=%async_computation.3 | async-start | bytes 1048576 | tf_op jit(solution)/shard_map/psum | solution.py:86
  86.0 1.0 copy-start.3
  86.0 0.7 copy-start.6
  87.3 0.7 copy-start.4
  88.0 0.7 copy-start.5
  126.4 0.7 copy-start.8
Sparse Core Ops, SparseCore 0:
  31.3 32.4 all-reduce.2
  86.1 31.5 all-reduce.4
